TPU v7x, 32 devices: a whole 2x2x4 slice. The times are simulated.
32 devices in a mesh: prow: 8 (over y, x, core), pcol: 4 (over z).
Axes of the slice: x: 2, y: 2, z: 4, core: 2. Of those that a mesh axis runs over, the one named last changes fastest.
Arguments:
- matrix: float32 [1024, 8192], P('prow', 'pcol'), as said below
- pivots: int32 [128], replicated, may hold values from 0 to 1023, as said below
Outputs:
- updated: float32 [1024, 8192], P('prow', 'pcol')
Inputs may be any that keep to these rules, and one draw needn't show every extreme that they name: pivots[j] is a logical row index from j to 1023; logical row i lies in row block i // 128, held by row process (i // 128) modulo the number of row processes. `matrix`: the strictly lower part of the panel's first 128 rows is small, so that L11 is well conditioned; entries of L21 are at most 1 in magnitude.
All inputs are finite; a program needn't handle non-finite values.
Results may differ from a plain program's by a relative error of at most 0.0003.
Values sent between devices are 32-bit elements; how exact they have to be, the bound alone decides.
A program may use at most 64 MiB of HBM per device.

v0:
```python
import functools

import jax
import jax.numpy as jnp
from jax import lax
from jax.experimental import pallas as pl
from jax.experimental.pallas import tpu as pltpu
from jax.sharding import PartitionSpec as P

MESH = pl.DeviceIdType.MESH
TOP_PIECES = 4
TILE = 256


def mm(a, b):
    return jnp.dot(a, b, preferred_element_type=jnp.float32)


def split(x):
    high = x.astype(jnp.bfloat16)
    low = (x - high.astype(jnp.float32)).astype(jnp.bfloat16)
    return high, low


def mm3(a, b):
    ah, al = split(a)
    bh, bl = split(b)
    return mm(ah, bh) + (mm(ah, bl) + mm(al, bh))


def kernel(
    procs, cols_procs, grid_x, a_ref, piv_ref, out_ref,
    abuf, top, hi, lo, cbuf, rbuf, gbuf, base, obuf, pan, l11, kbuf, proj,
    ex_sem, pz_send, pz_recv, pp_sem, l_send, l_recv, k_sem,
    rs_send, rs_recv, ag_send, ag_recv, t_send, t_recv, o_sem,
):
    B, cols = a_ref.shape
    half = cols // 2
    chips = procs // 2
    rc = B // chips
    rp = B // TOP_PIECES
    me = lax.axis_index("prow")
    z = lax.axis_index("pcol")
    chip = me // 2
    core = me % 2
    peer = chip * 2 + 1 - core

    def remote(src, dst, send, recv, device):
        return pltpu.make_async_remote_copy(
            src_ref=src, dst_ref=dst, send_sem=send, recv_sem=recv,
            device_id=device, device_id_type=MESH,
        )

    def snake(k):
        y, x = k // grid_x, k % grid_x
        odd = y % 2
        return y * grid_x + x + odd * (grid_x - 1 - 2 * x)

    def other(d):
        return (chip + d) % chips

    def rows_of(k):
        return pl.ds(pl.multiple_of(k * rc, rc), rc)

    barrier = pltpu.get_barrier_semaphore()
    greeted = [(peer, z)]
    greeted += [(other(d) * 2 + core, z) for d in range(1, chips)]
    greeted += [(me, (z + d) % cols_procs) for d in range(1, cols_procs)]
    for device in greeted:
        pl.semaphore_signal(barrier, inc=1, device_id=device, device_id_type=MESH)
    pl.semaphore_wait(barrier, len(greeted))

    mine = pl.ds(pl.multiple_of(core * half, half), half)
    theirs = pl.ds(pl.multiple_of((1 - core) * half, half), half)
    exchange = remote(
        a_ref.at[:, theirs], abuf.at[core], ex_sem.at[0], ex_sem.at[1], (peer, z)
    )
    exchange.start()

    panel_z = [
        remote(
            a_ref.at[:, pl.ds(0, B)], pan.at[core],
            pz_send.at[d - 1], pz_recv.at[0], (me, (z + d) % cols_procs),
        )
        for d in range(1, cols_procs)
    ]

    @pl.when(z == 0)
    def _():
        for copy in panel_z:
            copy.start()
        pan[core] = a_ref[:, :B]

    row = lax.broadcasted_iota(jnp.int32, (B, B), 0)
    col = lax.broadcasted_iota(jnp.int32, (B, B), 1)
    eye = row == col
    piv = piv_ref[...]
    pr = jnp.broadcast_to(piv, (B, B))
    pc = jnp.sum(jnp.where(eye, pr, 0), axis=1, keepdims=True)
    colf = col.astype(jnp.float32)
    before = col < row

    def last(mask, lanes):
        return jnp.max(jnp.where(mask, lanes, -1.0), axis=1, keepdims=True)

    prev = last((pc == pr) & before, colf)
    parent = last((pr == row) & before, colf)
    root_self = parent < 0
    hot = jnp.where(
        root_self, jnp.where(eye, 1.0, 0.0), jnp.where(colf == parent, 1.0, 0.0)
    ).astype(jnp.bfloat16)
    steps = 1
    while steps < B:
        hot = mm(hot, hot).astype(jnp.bfloat16)
        steps *= 2
    from_prev = mm(jnp.where(colf == prev, 1.0, 0.0).astype(jnp.bfloat16), hot)

    first = chip * (2 * B)
    col2 = lax.broadcasted_iota(jnp.int32, (B, 2 * B), 1)
    on_first = (chip == 0).astype(jnp.float32)
    direct = jnp.where((prev < 0) & (pc == col2 + first), 1.0, 0.0)
    pick = jnp.concatenate(
        [direct[:, :B] + on_first * from_prev, direct[:, B:]], axis=1
    ).astype(jnp.bfloat16)

    row2 = lax.broadcasted_iota(jnp.int32, (2 * B, B), 0)
    col3 = lax.broadcasted_iota(jnp.int32, (2 * B, B), 1).astype(jnp.float32)
    logical = row2 + first
    filled = last(jnp.broadcast_to(piv, (2 * B, B)) == logical, col3)
    is_rest = logical[:, :1] >= B
    fill = jnp.where((col3 == filled) & (logical >= B), 1.0, 0.0)
    fill = mm(fill.astype(jnp.bfloat16), hot).astype(jnp.bfloat16)
    keep = jnp.where(is_rest & (filled < 0), 1.0, 0.0)

    own_rows = pl.ds(pl.multiple_of(core * B, B), B)
    peer_rows = pl.ds(pl.multiple_of((1 - core) * B, B), B)
    h, l = split(a_ref[:, mine])
    hi[own_rows, :] = h
    lo[own_rows, :] = l

    step = 1 - 2 * core
    place = snake(chip)
    rank = (place * step + chips) % chips
    onward = snake((place + step + chips) % chips) * 2 + core
    top_copies = [
        remote(
            top.at[pl.ds(i * rp, rp)], top.at[pl.ds(i * rp, rp)],
            t_send.at[i], t_recv.at[i], (onward, z),
        )
        for i in range(TOP_PIECES)
    ]

    @pl.when(me == 0)
    def _():
        top[...] = a_ref[:, :half]

    exchange.wait_recv()

    @pl.when(me == 1)
    def _():
        top[...] = abuf[0]

    @pl.when(chip == 0)
    def _():
        for copy in top_copies:
            copy.start()

    h, l = split(abuf[1 - core])
    hi[peer_rows, :] = h
    lo[peer_rows, :] = l

    to_zero = remote(pan.at[core], pan.at[core], pp_sem.at[0], pp_sem.at[1], (peer, z))
    l_copies = [
        remote(pan.at[0], l11, l_send.at[d - 1], l_recv.at[0], (other(d) * 2 + core, z))
        for d in range(1, chips)
    ]

    @pl.when(z != 0)
    def _():
        panel_z[0].wait_recv()

    @pl.when(core == 1)
    def _():
        to_zero.start()

    @pl.when(me == 0)
    def _():
        for copy in l_copies:
            copy.start()
        l11[...] = pan[0]

    for t in range(0, half, TILE):
        s = pl.ds(t, TILE)
        cbuf[:, s] = mm(pick, hi[:, s]) + mm(pick, lo[:, s])
    rs = [
        remote(
            cbuf.at[rows_of(other(d))], rbuf.at[d - 1],
            rs_send.at[d - 1], rs_recv.at[d - 1], (other(d) * 2 + core, z),
        )
        for d in range(1, chips)
    ]
    for copy in rs:
        copy.start()

    def forward(i):
        @pl.when(rank > 0)
        def _():
            top_copies[i].wait_recv()

        @pl.when((rank > 0) & (rank < chips - 1))
        def _():
            top_copies[i].start()

    proj[:, :] = fill

    forward(0)

    @pl.when((core == 0) & (chip != 0))
    def _():
        l_copies[0].wait_recv()

    @pl.when(core == 0)
    def _():
        to_zero.wait_recv()

    levels = []
    size = 2
    while size < B:
        levels.append(size)
        size *= 2

    def off_diagonal(size):
        same = (row & (-2 * size)) == (col & (-2 * size))
        return jnp.where(
            same & ((row & size) != 0) & ((col & size) == 0), l11[...], 0.0
        )

    def advance(sizes):
        @pl.when(core == 0)
        def _():
            x = kbuf[:B, :]
            for size in sizes:
                x = x - mm3(x, mm3(off_diagonal(size), x))
            kbuf[:B, :] = x

    @pl.when(core == 0)
    def _():
        kbuf[:B, :] = jnp.where(eye, 1.0, 0.0) - off_diagonal(1)

    at = 0
    for i in range(1, TOP_PIECES):
        upto = len(levels) * i // (TOP_PIECES - 1)
        advance(levels[at:upto])
        at = upto
        forward(i)

    k_copy = remote(kbuf, kbuf, k_sem.at[0], k_sem.at[1], (peer, z))

    @pl.when(core == 0)
    def _():
        inverse = kbuf[:B, :]
        lead = on_first * jnp.where(eye, 1.0, 0.0) - (1.0 - on_first) * pan[0]
        low_part = mm3(pan[1], inverse)
        kbuf[:B, :] = mm3(lead, inverse)
        kbuf[B:, :] = -low_part
        k_copy.start()

    for copy in rs:
        copy.wait_recv()
    total = cbuf[rows_of(chip), :]
    for d in range(1, chips):
        total = total + rbuf[d - 1]
    gbuf[rows_of(chip), :] = total
    ag = [
        remote(
            gbuf.at[rows_of(chip)], gbuf.at[rows_of(chip)],
            ag_send.at[d - 1], ag_recv.at[d - 1], (other(d) * 2 + core, z),
        )
        for d in range(1, chips)
    ]
    for copy in ag:
        copy.start()

    own_keep = jnp.where(core == 0, keep[:B], keep[B:])
    peer_keep = jnp.where(core == 0, keep[B:], keep[:B])
    base[own_rows, :] = own_keep * a_ref[:, mine]
    base[peer_rows, :] = peer_keep * abuf[1 - core]
    for t in range(0, half, TILE):
        s = pl.ds(t, TILE)
        th, tl = split(top[:, s])
        base[:, s] = base[:, s] + (mm(proj[...], th) + mm(proj[...], tl))

    @pl.when(core == 1)
    def _():
        k_copy.wait_recv()

    kh_peer, kl_peer = split(kbuf[peer_rows, :])
    kh_own, kl_own = split(kbuf[own_rows, :])
    for d in range(1, chips):
        came = (chip - d + chips) % chips
        remote(
            gbuf.at[rows_of(came)], gbuf.at[rows_of(came)],
            ag_send.at[d - 1], ag_recv.at[d - 1], (other(d) * 2 + core, z),
        ).wait_recv()

    out_peer = remote(obuf.at[0], out_ref.at[:, mine], o_sem.at[0], o_sem.at[1], (peer, z))
    out_own = pltpu.make_async_copy(obuf.at[1], out_ref.at[:, mine], o_sem.at[2])
    for t in range(0, half, TILE):
        s = pl.ds(t, TILE)
        gh, gl = split(gbuf[:, s])
        obuf[0, :, s] = base[peer_rows, s] + (
            mm(kh_peer, gh) + (mm(kh_peer, gl) + mm(kl_peer, gh))
        )
    out_peer.start()
    for t in range(0, half, TILE):
        s = pl.ds(t, TILE)
        gh, gl = split(gbuf[:, s])
        obuf[1, :, s] = base[own_rows, s] + (
            mm(kh_own, gh) + (mm(kh_own, gl) + mm(kl_own, gh))
        )
    out_own.start()

    exchange.wait_send()

    @pl.when(z == 0)
    def _():
        for copy in panel_z:
            copy.wait_send()

    @pl.when(core == 1)
    def _():
        to_zero.wait_send()

    @pl.when(core == 0)
    def _():
        k_copy.wait_send()

    @pl.when(me == 0)
    def _():
        for copy in l_copies:
            copy.wait_send()

    @pl.when(rank < chips - 1)
    def _():
        for copy in top_copies:
            copy.wait_send()

    for copy in rs + ag:
        copy.wait_send()
    out_own.wait()
    remote(
        obuf.at[0], out_ref.at[:, theirs], o_sem.at[0], o_sem.at[1], (peer, z)
    ).wait_recv()
    out_peer.wait_send()


def local(procs, cols_procs, matrix, pivots):
    B, cols = matrix.shape
    half = cols // 2
    chips = procs // 2
    grid_x = 1
    while (grid_x * 2) * (grid_x * 2) <= chips:
        grid_x *= 2
    f32, bf16 = jnp.float32, jnp.bfloat16
    dma = pltpu.SemaphoreType.DMA
    stepped = pl.pallas_call(
        functools.partial(kernel, procs, cols_procs, grid_x),
        out_shape=jax.ShapeDtypeStruct((B, cols), f32),
        in_specs=[pl.BlockSpec(memory_space=pltpu.VMEM)] * 2,
        out_specs=pl.BlockSpec(memory_space=pl.ANY),
        scratch_shapes=[
            pltpu.VMEM((2, B, half), f32),
            pltpu.VMEM((B, half), f32),
            pltpu.VMEM((2 * B, half), bf16),
            pltpu.VMEM((2 * B, half), bf16),
            pltpu.VMEM((B, half), f32),
            pltpu.VMEM((chips - 1, B // chips, half), f32),
            pltpu.VMEM((B, half), f32),
            pltpu.VMEM((2 * B, half), f32),
            pltpu.VMEM((2, B, half), f32),
            pltpu.VMEM((2, B, B), f32),
            pltpu.VMEM((B, B), f32),
            pltpu.VMEM((2 * B, B), f32),
            pltpu.VMEM((2 * B, B), bf16),
            dma((2,)),
            dma((cols_procs - 1,)),
            dma((1,)),
            dma((2,)),
            dma((chips - 1,)),
            dma((1,)),
            dma((2,)),
            dma((chips - 1,)),
            dma((chips - 1,)),
            dma((chips - 1,)),
            dma((chips - 1,)),
            dma((TOP_PIECES,)),
            dma((TOP_PIECES,)),
            dma((3,)),
        ],
        compiler_params=pltpu.CompilerParams(
            collective_id=0, has_side_effects=True, vmem_limit_bytes=32 * 1024 * 1024
        ),
    )(matrix, pivots.reshape(1, -1))
    col_ids = jnp.arange(cols, dtype=jnp.int32)
    keep_panel = (lax.axis_index("pcol") == 0) & (col_ids < pivots.shape[0])
    return jnp.where(keep_panel[None, :], matrix, stepped)


def solution(mesh):
    body = functools.partial(local, mesh.shape["prow"], mesh.shape["pcol"])
    return jax.shard_map(
        body, mesh=mesh, in_specs=(P("prow", "pcol"), P()),
        out_specs=P("prow", "pcol"), check_vma=False,
    )
```

profile of v0, /device:TPU:19, one launch (start us, length us, event | category | flops | bytes accessed | tf_op | source)
XLA Modules:
  0.0 44.1 jit_solution(16088189010030758270)
XLA Ops:
  0.0 0.0 copy-start.1
  0.0 0.6 %copy-done.1 = s32[128]{0:T(128)S(1)} copy-done((s32[128]{0:T(128)S(1)}, s32[128]{0:T(128)}, u32[]{:S(2)}) %copy-start.1) | copy-done | bytes 536
  0.7 0.0 copy-start
  0.7 1.2 %copy-done = f32[128,2048]{1,0:T(8,128)S(1)} copy-done((f32[128,2048]{1,0:T(8,128)S(1)}, f32[128,2048]{1,0:T(8,128)}, u32[]{:S(2)}) %copy-start) | copy-done | bytes 1048600
  1.9 41.1 %shard_map.28 = f32[128,2048]{1,0:T(8,128)S(1)} custom-call(f32[128,2048]{1,0:T(8,128)S(1)} %copy-done, s32[1,128]{1,0:T(1,128)S(1)} %bitcast.1), custom_call_target="tpu_custom_call" | custom-call | tf_op jit(solution)/shard_map/pallas_call | solution.py:366
  42.9 1.1 %broadcast_select_fusion = f32[128,2048]{1,0:T(8,128)} fusion(f32[128,2048]{1,0:T(8,128)S(1)} %copy-done, f32[128,2048]{1,0:T(8,128)S(1)} %shard_map.28, pred[2048]{0:T(1024)(128)(4,1)S(1)} %fusion), kind=kLoop, calls=%fused_computation | loop fusion | flops 262144 | bytes 3147776 | tf_op jit(solution)/shard_map/jit(_where)/select_n | solution.py:406
  (1 shorter events, 0.0 us)
Async XLA Ops:
  0.0 0.7 %copy-start.1 = (s32[128]{0:T(128)S(1)}, s32[128]{0:T(128)}, u32[]{:S(2)}) copy-start(s32[128]{0:T(128)} %param.3) | copy-start | bytes 1540
  0.7 1.2 %copy-start = (f32[128,2048]{1,0:T(8,128)S(1)}, f32[128,2048]{1,0:T(8,128)}, u32[]{:S(2)}) copy-start(f32[128,2048]{1,0:T(8,128)} %a_ref.1) | copy-start | bytes 3145732
where the time goes:
time: 44.2 us; the launch traced here: 44.1 us
  Pallas kernels  41.1 us (93%)
  local copies, waits for them, and re-layouts  1.87 us (4%)
  other arithmetic  1.13 us (3%)
    pallas_call x1, Pallas kernels, local(): pl.pallas_call(functools.partial(kernel, procs, cols_procs, grid_x), out_...  41.1 us
    unnamed x4, local copies, waits for them, and re-layouts  1.87 us
    select_n x1, other arithmetic, local(): return jnp.where(keep_panel[None, :], matrix, stepped)  1.12 us

commit v1 on v0

v1 whole, which is shorter than its diff:
```python
import functools

import jax
import jax.numpy as jnp
from jax import lax
from jax.experimental import pallas as pl
from jax.experimental.pallas import tpu as pltpu
from jax.sharding import PartitionSpec as P

MESH = pl.DeviceIdType.MESH
TOP_PIECES = 4
EARLY = 2
TILE = 256


def mm(a, b):
    return jnp.dot(a, b, preferred_element_type=jnp.float32)


def split(x):
    high = x.astype(jnp.bfloat16)
    low = (x - high.astype(jnp.float32)).astype(jnp.bfloat16)
    return high, low


def mm3(a, b):
    ah, al = split(a)
    bh, bl = split(b)
    return mm(ah, bh) + (mm(ah, bl) + mm(al, bh))


def kernel(
    procs, cols_procs, grid_x, a_ref, piv_ref, out_ref,
    abuf, top, hi, lo, cbuf, rbuf, hbuf, qbuf, gbuf, base, obuf, pan, l11, kbuf, proj,
    in_sem, ex_sem, pz_send, pz_recv, pp_sem, l_send, l_recv, k_sem,
    rs_send, rs_recv, hs_send, hs_recv, ag_send, ag_recv, fw_send, fw_recv,
    t_send, t_recv, p_send, p_recv, o_sem,
):
    B, cols = a_ref.shape
    half = cols // 2
    chips = procs // 2
    rc = B // chips
    rp = B // TOP_PIECES
    me = lax.axis_index("prow")
    z = lax.axis_index("pcol")
    chip = me // 2
    core = me % 2
    peer = chip * 2 + 1 - core

    def remote(src, dst, send, recv, device):
        return pltpu.make_async_remote_copy(
            src_ref=src, dst_ref=dst, send_sem=send, recv_sem=recv,
            device_id=device, device_id_type=MESH,
        )

    def snake(k):
        across, down = k % grid_x, k // grid_x
        return down * grid_x + across + down % 2 * (grid_x - 1 - 2 * across)

    n = grid_x
    y, x = chip // n, chip % n
    u = x + core * (y - x)
    v = y + core * (x - y)

    def at_uv(uu, vv):
        return (uu + core * (vv - uu)) + n * (vv + core * (uu - vv))

    def along_u(d):
        return at_uv((u + d) % n, v) * 2 + core, z

    def along_v(d):
        return at_uv(u, (v + d) % n) * 2 + core, z

    def rows_of(k, count=1):
        return pl.ds(pl.multiple_of(k * rc, rc), count * rc)

    mine = pl.ds(pl.multiple_of(core * half, half), half)
    theirs = pl.ds(pl.multiple_of((1 - core) * half, half), half)
    load = pltpu.make_async_copy(a_ref.at[:, mine], abuf.at[core], in_sem.at[0])
    load.start()
    load_panel = pltpu.make_async_copy(
        a_ref.at[:, pl.ds(0, B)], pan.at[core], in_sem.at[1]
    )

    @pl.when(z == 0)
    def _():
        load_panel.start()

    step = 1 - 2 * core
    place = snake(chip)
    rank = (place * step + chips) % chips
    onward = snake((place + step + chips) % chips) * 2 + core
    behind = snake((place - step + chips) % chips) * 2 + core

    barrier = pltpu.get_barrier_semaphore()
    greeted = [(peer, z)]
    greeted += [along_u(d) for d in range(1, n)]
    greeted += [along_v(d) for d in range(1, n)]
    greeted += [(onward, z), (behind, z)] if n > 2 else []
    greeted += [(me, (z + d) % cols_procs) for d in range(1, cols_procs)]
    for device in greeted:
        pl.semaphore_signal(barrier, inc=1, device_id=device, device_id_type=MESH)

    row = lax.broadcasted_iota(jnp.int32, (B, B), 0)
    col = lax.broadcasted_iota(jnp.int32, (B, B), 1)
    eye = row == col
    piv = piv_ref[...]
    pr = jnp.broadcast_to(piv, (B, B))
    pc = jnp.sum(jnp.where(eye, pr, 0), axis=1, keepdims=True)
    colf = col.astype(jnp.float32)
    before = col < row

    def last(mask, lanes):
        return jnp.max(jnp.where(mask, lanes, -1.0), axis=1, keepdims=True)

    prev = last((pc == pr) & before, colf)
    parent = last((pr == row) & before, colf)
    root_self = parent < 0
    hot = jnp.where(
        root_self, jnp.where(eye, 1.0, 0.0), jnp.where(colf == parent, 1.0, 0.0)
    ).astype(jnp.bfloat16)
    pl.semaphore_wait(barrier, len(greeted))

    exchange = remote(
        a_ref.at[:, theirs], abuf.at[core], ex_sem.at[0], ex_sem.at[1], (peer, z)
    )
    exchange.start()

    panel_z = [
        remote(
            a_ref.at[:, pl.ds(0, B)], pan.at[core],
            pz_send.at[d - 1], pz_recv.at[0], (me, (z + d) % cols_procs),
        )
        for d in range(1, cols_procs)
    ]

    @pl.when(z == 0)
    def _():
        for copy in panel_z:
            copy.start()

    top_copies = [
        remote(
            top.at[pl.ds(i * rp, rp)], top.at[pl.ds(i * rp, rp)],
            t_send.at[i], t_recv.at[i], (onward, z),
        )
        for i in range(TOP_PIECES)
    ]

    load.wait()

    @pl.when(me == 0)
    def _():
        top[...] = abuf[0]
        for copy in top_copies[:EARLY]:
            copy.start()

    steps = 1
    while steps < B:
        hot = mm(hot, hot).astype(jnp.bfloat16)
        steps *= 2
    from_prev = mm(jnp.where(colf == prev, 1.0, 0.0).astype(jnp.bfloat16), hot)

    first = chip * (2 * B)
    col2 = lax.broadcasted_iota(jnp.int32, (B, 2 * B), 1)
    on_first = (chip == 0).astype(jnp.float32)
    direct = jnp.where((prev < 0) & (pc == col2 + first), 1.0, 0.0)
    pick = jnp.concatenate(
        [direct[:, :B] + on_first * from_prev, direct[:, B:]], axis=1
    ).astype(jnp.bfloat16)

    row2 = lax.broadcasted_iota(jnp.int32, (2 * B, B), 0)
    col3 = lax.broadcasted_iota(jnp.int32, (2 * B, B), 1).astype(jnp.float32)
    logical = row2 + first
    filled = last(jnp.broadcast_to(piv, (2 * B, B)) == logical, col3)
    is_rest = logical[:, :1] >= B
    fill = jnp.where((col3 == filled) & (logical >= B), 1.0, 0.0)
    fill = mm(fill.astype(jnp.bfloat16), hot).astype(jnp.bfloat16)
    keep = jnp.where(is_rest & (filled < 0), 1.0, 0.0)

    own_rows = pl.ds(pl.multiple_of(core * B, B), B)
    peer_rows = pl.ds(pl.multiple_of((1 - core) * B, B), B)
    h, l = split(abuf[core])
    hi[own_rows, :] = h
    lo[own_rows, :] = l

    exchange.wait_recv()

    @pl.when(me == 1)
    def _():
        top[...] = abuf[0]
        for copy in top_copies[:EARLY]:
            copy.start()

    h, l = split(abuf[1 - core])
    hi[peer_rows, :] = h
    lo[peer_rows, :] = l

    to_zero = remote(pan.at[core], pan.at[core], pp_sem.at[0], pp_sem.at[1], (peer, z))
    l_first = [
        remote(pan.at[0], l11, l_send.at[d - 1], l_recv.at[0], along_u(d))
        for d in range(1, n)
    ]
    l_then = [
        remote(l11, l11, l_send.at[n - 2 + d], l_recv.at[0], along_v(d))
        for d in range(1, n)
    ]

    @pl.when(z != 0)
    def _():
        panel_z[0].wait_recv()

    @pl.when(z == 0)
    def _():
        load_panel.wait()

    @pl.when(core == 1)
    def _():
        to_zero.start()

    @pl.when(me == 0)
    def _():
        for copy in l_first:
            copy.start()
        l11[...] = pan[0]
        for copy in l_then:
            copy.start()

    for t in range(0, half, TILE):
        s = pl.ds(t, TILE)
        cbuf[:, s] = mm(pick, hi[:, s]) + mm(pick, lo[:, s])
    rs = [
        remote(
            cbuf.at[rows_of((u + d) % n * n, n)], rbuf.at[d - 1],
            rs_send.at[d - 1], rs_recv.at[d - 1], along_u(d),
        )
        for d in range(1, n)
    ]
    for copy in rs:
        copy.start()

    @pl.when(rank == 0)
    def _():
        for copy in top_copies[EARLY:]:
            copy.start()

    def forward(i):
        @pl.when((rank > 0) & (rank < chips - 1))
        def _():
            top_copies[i].wait_recv()
            top_copies[i].start()

    proj[:, :] = fill

    forward(0)

    @pl.when((core == 0) & (chip != 0))
    def _():
        l_first[0].wait_recv()

    @pl.when((core == 0) & (chip != 0) & (y == 0))
    def _():
        for copy in l_then:
            copy.start()

    @pl.when(core == 0)
    def _():
        to_zero.wait_recv()

    levels = []
    size = 2
    while size < B:
        levels.append(size)
        size *= 2

    def off_diagonal(size):
        same = (row & (-2 * size)) == (col & (-2 * size))
        return jnp.where(
            same & ((row & size) != 0) & ((col & size) == 0), l11[...], 0.0
        )

    def advance(sizes):
        @pl.when(core == 0)
        def _():
            x = kbuf[:B, :]
            for size in sizes:
                x = x - mm3(x, mm3(off_diagonal(size), x))
            kbuf[:B, :] = x

    @pl.when(core == 0)
    def _():
        kbuf[:B, :] = jnp.where(eye, 1.0, 0.0) - off_diagonal(1)

    cut = (len(levels) + 1) // 3
    advance(levels[:cut])
    for copy in rs:
        copy.wait_recv()
    total = cbuf[rows_of(u * n, n), :]
    for d in range(1, n):
        total = total + rbuf[d - 1]
    hbuf[...] = total
    hs = [
        remote(
            hbuf.at[rows_of((v + d) % n)], qbuf.at[d - 1],
            hs_send.at[d - 1], hs_recv.at[d - 1], along_v(d),
        )
        for d in range(1, n)
    ]
    for copy in hs:
        copy.start()
    forward(1)
    advance(levels[cut : 2 * cut])
    for copy in hs:
        copy.wait_recv()
    total = hbuf[rows_of(v), :]
    for d in range(1, n):
        total = total + qbuf[d - 1]
    own_chunk = rows_of(u * n + v)
    gbuf[own_chunk, :] = total

    ag = [
        remote(
            gbuf.at[own_chunk], gbuf.at[own_chunk],
            ag_send.at[d - 1], ag_recv.at[d - 1], along_v(d),
        )
        for d in range(1, n)
    ]
    fw = []
    for e in range(n):
        chunk = rows_of(u * n + (v - e + n) % n)
        fw.append([
            remote(
                gbuf.at[chunk], gbuf.at[chunk],
                fw_send.at[e * (n - 1) + d - 1], fw_recv.at[e * (n - 1) + d - 1],
                along_u(d),
            )
            for d in range(1, n)
        ])
    for copy in ag + fw[0]:
        copy.start()
    for i in range(2, TOP_PIECES):
        forward(i)
    advance(levels[2 * cut :])
    for e in range(1, n):
        chunk = rows_of(u * n + (v - e + n) % n)
        remote(
            gbuf.at[chunk], gbuf.at[chunk],
            ag_send.at[e - 1], ag_recv.at[e - 1], along_v(e),
        ).wait_recv()
        for copy in fw[e]:
            copy.start()

    k_copy = remote(kbuf, kbuf, k_sem.at[0], k_sem.at[1], (peer, z))

    @pl.when(core == 0)
    def _():
        inverse = kbuf[:B, :]
        lead = on_first * jnp.where(eye, 1.0, 0.0) - (1.0 - on_first) * pan[0]
        low_part = mm3(pan[1], inverse)
        kbuf[:B, :] = mm3(lead, inverse)
        kbuf[B:, :] = -low_part
        k_copy.start()

    @pl.when(rank == chips - 1)
    def _():
        for copy in top_copies:
            copy.wait_recv()

    base[:B, :] = keep[:B] * abuf[0]
    base[B:, :] = keep[B:] * abuf[1]
    for t in range(0, half, TILE):
        s = pl.ds(t, TILE)
        th, tl = split(top[:, s])
        base[:, s] = base[:, s] + (mm(proj[...], th) + mm(proj[...], tl))

    @pl.when(core == 1)
    def _():
        k_copy.wait_recv()

    kh_peer, kl_peer = split(kbuf[peer_rows, :])
    kh_own, kl_own = split(kbuf[own_rows, :])
    for e in range(n):
        for d in range(1, n):
            chunk = rows_of((u - d + n) % n * n + (v - e + n) % n)
            remote(
                gbuf.at[chunk], gbuf.at[chunk],
                fw_send.at[e * (n - 1) + d - 1], fw_recv.at[e * (n - 1) + d - 1],
                along_u(d),
            ).wait_recv()

    def tile_of(side, t):
        return pl.ds(pl.multiple_of(side * half + t, TILE), TILE)

    tiles = range(0, half, TILE)
    out_peer = [
        remote(
            obuf.at[0, :, pl.ds(t, TILE)], out_ref.at[:, tile_of(core, t)],
            p_send.at[t // TILE], p_recv.at[t // TILE], (peer, z),
        )
        for t in tiles
    ]
    out_own = pltpu.make_async_copy(obuf.at[1], out_ref.at[:, mine], o_sem.at[0])
    for t in tiles:
        s = pl.ds(t, TILE)
        gh, gl = split(gbuf[:, s])
        obuf[0, :, s] = base[peer_rows, s] + (
            mm(kh_peer, gh) + (mm(kh_peer, gl) + mm(kl_peer, gh))
        )
        out_peer[t // TILE].start()
    for t in tiles:
        s = pl.ds(t, TILE)
        gh, gl = split(gbuf[:, s])
        obuf[1, :, s] = base[own_rows, s] + (
            mm(kh_own, gh) + (mm(kh_own, gl) + mm(kl_own, gh))
        )
    out_own.start()

    exchange.wait_send()

    @pl.when(z == 0)
    def _():
        for copy in panel_z:
            copy.wait_send()

    @pl.when(core == 1)
    def _():
        to_zero.wait_send()

    @pl.when(core == 0)
    def _():
        k_copy.wait_send()

    @pl.when(me == 0)
    def _():
        for copy in l_first:
            copy.wait_send()

    @pl.when((core == 0) & (y == 0))
    def _():
        for copy in l_then:
            copy.wait_send()

    @pl.when(rank < chips - 1)
    def _():
        for copy in top_copies:
            copy.wait_send()

    for copy in rs + hs + ag + [c for part in fw for c in part]:
        copy.wait_send()
    out_own.wait()
    for t in tiles:
        remote(
            obuf.at[0, :, pl.ds(t, TILE)], out_ref.at[:, tile_of(1 - core, t)],
            p_send.at[t // TILE], p_recv.at[t // TILE], (peer, z),
        ).wait_recv()
    for copy in out_peer:
        copy.wait_send()


def local(procs, cols_procs, matrix, pivots):
    B, cols = matrix.shape
    half = cols // 2
    chips = procs // 2
    n = 1
    while n * n < chips:
        n += 1
    f32, bf16 = jnp.float32, jnp.bfloat16
    dma = pltpu.SemaphoreType.DMA
    stepped = pl.pallas_call(
        functools.partial(kernel, procs, cols_procs, n),
        out_shape=jax.ShapeDtypeStruct((B, cols), f32),
        in_specs=[
            pl.BlockSpec(memory_space=pltpu.HBM),
            pl.BlockSpec(memory_space=pltpu.VMEM),
        ],
        out_specs=pl.BlockSpec(memory_space=pl.ANY),
        scratch_shapes=[
            pltpu.VMEM((2, B, half), f32),
            pltpu.VMEM((B, half), f32),
            pltpu.VMEM((2 * B, half), bf16),
            pltpu.VMEM((2 * B, half), bf16),
            pltpu.VMEM((B, half), f32),
            pltpu.VMEM((n - 1, B // n, half), f32),
            pltpu.VMEM((B // n, half), f32),
            pltpu.VMEM((n - 1, B // chips, half), f32),
            pltpu.VMEM((B, half), f32),
            pltpu.VMEM((2 * B, half), f32),
            pltpu.VMEM((2, B, half), f32),
            pltpu.VMEM((2, B, B), f32),
            pltpu.VMEM((B, B), f32),
            pltpu.VMEM((2 * B, B), f32),
            pltpu.VMEM((2 * B, B), bf16),
            dma((2,)),
            dma((2,)),
            dma((cols_procs - 1,)),
            dma((1,)),
            dma((2,)),
            dma((2 * (n - 1),)),
            dma((1,)),
            dma((2,)),
            dma((n - 1,)),
            dma((n - 1,)),
            dma((n - 1,)),
            dma((n - 1,)),
            dma((n - 1,)),
            dma((n - 1,)),
            dma((n * (n - 1),)),
            dma((n * (n - 1),)),
            dma((TOP_PIECES,)),
            dma((TOP_PIECES,)),
            dma((half // TILE,)),
            dma((half // TILE,)),
            dma((1,)),
        ],
        compiler_params=pltpu.CompilerParams(
            collective_id=0, has_side_effects=True, vmem_limit_bytes=60 * 1024 * 1024
        ),
    )(matrix, pivots.reshape(1, -1))
    col_ids = jnp.arange(cols, dtype=jnp.int32)
    keep_panel = (lax.axis_index("pcol") == 0) & (col_ids < pivots.shape[0])
    return jnp.where(keep_panel[None, :], matrix, stepped)


def solution(mesh):
    body = functools.partial(local, mesh.shape["prow"], mesh.shape["pcol"])
    return jax.shard_map(
        body, mesh=mesh, in_specs=(P("prow", "pcol"), P()),
        out_specs=P("prow", "pcol"), check_vma=False,
    )
```

time: 44.2 us -> 38.7 us (0.88)
  the two profiles are of different devices: /device:TPU:19 before, /device:TPU:29 now
where the time goes in v1:
time: 38.7 us; the launch traced here: 38.6 us
  Pallas kernels  36.2 us (94%)
  other arithmetic  2.34 us (6%)
    pallas_call x1, Pallas kernels, local(): pl.pallas_call(functools.partial(kernel, procs, cols_procs, n), out_shape...  36.2 us
    select_n x1, other arithmetic, local(): return jnp.where(keep_panel[None, :], matrix, stepped)  2.33 us

profile of v1, /device:TPU:29, one launch (start us, length us, event | category | flops | bytes accessed | tf_op | source)
XLA Modules:
  0.0 38.6 jit_solution(5570467105848708526)
XLA Ops:
  0.0 0.0 copy-start
  0.0 36.2 %shard_map.28 = f32[128,2048]{1,0:T(8,128)} custom-call(f32[128,2048]{1,0:T(8,128)} %a_ref.1, s32[1,128]{1,0:T(1,128)} %bitcast.1), custom_call_target="tpu_custom_call" | custom-call | tf_op jit(solution)/shard_map/pallas_call | solution.py:469
  36.2 0.0 copy-done
  36.2 2.3 %broadcast_select_fusion = f32[128,2048]{1,0:T(8,128)} fusion(f32[128,2048]{1,0:T(8,128)S(1)} %copy-done, f32[128,2048]{1,0:T(8,128)} %shard_map.28, pred[2048]{0:T(1024)(128)(4,1)S(1)} %fusion), kind=kLoop, calls=%fused_computation | loop fusion | flops 262144 | bytes 3147776 | tf_op jit(solution)/shard_map/jit(_where)/select_n | solution.py:521
  (1 shorter events, 0.0 us)
Async XLA Ops:
  0.0 36.2 %copy-start = (f32[128,2048]{1,0:T(8,128)S(1)}, f32[128,2048]{1,0:T(8,128)}, u32[]{:S(2)}) copy-start(f32[128,2048]{1,0:T(8,128)} %a_ref.1) | copy-start | bytes 3145732

commit v2 on v1

--- a/solution.py
+++ b/solution.py
@@ -31,9 +31,9 @@
 
 def kernel(
     procs, cols_procs, grid_x, a_ref, piv_ref, out_ref,
-    abuf, top, hi, lo, cbuf, rbuf, hbuf, qbuf, gbuf, base, obuf, pan, l11, kbuf, proj,
+    abuf, top, hi, lo, cbuf, rbuf, gbuf, base, obuf, pan, l11, kbuf, proj,
     in_sem, ex_sem, pz_send, pz_recv, pp_sem, l_send, l_recv, k_sem,
-    rs_send, rs_recv, hs_send, hs_recv, ag_send, ag_recv, fw_send, fw_recv,
+    rs_send, rs_recv, ag_send, ag_recv,
     t_send, t_recv, p_send, p_recv, o_sem,
 ):
     B, cols = a_ref.shape
@@ -57,22 +57,11 @@
         across, down = k % grid_x, k // grid_x
         return down * grid_x + across + down % 2 * (grid_x - 1 - 2 * across)
 
-    n = grid_x
-    y, x = chip // n, chip % n
-    u = x + core * (y - x)
-    v = y + core * (x - y)
-
-    def at_uv(uu, vv):
-        return (uu + core * (vv - uu)) + n * (vv + core * (uu - vv))
-
-    def along_u(d):
-        return at_uv((u + d) % n, v) * 2 + core, z
-
-    def along_v(d):
-        return at_uv(u, (v + d) % n) * 2 + core, z
-
-    def rows_of(k, count=1):
-        return pl.ds(pl.multiple_of(k * rc, rc), count * rc)
+    def other(d):
+        return (chip + d) % chips
+
+    def rows_of(k):
+        return pl.ds(pl.multiple_of(k * rc, rc), rc)
 
     mine = pl.ds(pl.multiple_of(core * half, half), half)
     theirs = pl.ds(pl.multiple_of((1 - core) * half, half), half)
@@ -90,13 +79,10 @@
     place = snake(chip)
     rank = (place * step + chips) % chips
     onward = snake((place + step + chips) % chips) * 2 + core
-    behind = snake((place - step + chips) % chips) * 2 + core
 
     barrier = pltpu.get_barrier_semaphore()
     greeted = [(peer, z)]
-    greeted += [along_u(d) for d in range(1, n)]
-    greeted += [along_v(d) for d in range(1, n)]
-    greeted += [(onward, z), (behind, z)] if n > 2 else []
+    greeted += [(other(d) * 2 + core, z) for d in range(1, chips)]
     greeted += [(me, (z + d) % cols_procs) for d in range(1, cols_procs)]
     for device in greeted:
         pl.semaphore_signal(barrier, inc=1, device_id=device, device_id_type=MESH)
@@ -197,44 +183,20 @@
     lo[peer_rows, :] = l
 
     to_zero = remote(pan.at[core], pan.at[core], pp_sem.at[0], pp_sem.at[1], (peer, z))
-    l_first = [
-        remote(pan.at[0], l11, l_send.at[d - 1], l_recv.at[0], along_u(d))
-        for d in range(1, n)
-    ]
-    l_then = [
-        remote(l11, l11, l_send.at[n - 2 + d], l_recv.at[0], along_v(d))
-        for d in range(1, n)
-    ]
-
-    @pl.when(z != 0)
-    def _():
-        panel_z[0].wait_recv()
-
-    @pl.when(z == 0)
-    def _():
-        load_panel.wait()
-
-    @pl.when(core == 1)
-    def _():
-        to_zero.start()
-
-    @pl.when(me == 0)
-    def _():
-        for copy in l_first:
-            copy.start()
-        l11[...] = pan[0]
-        for copy in l_then:
-            copy.start()
+    l_copies = [
+        remote(pan.at[0], l11, l_send.at[d - 1], l_recv.at[0], (other(d) * 2 + core, z))
+        for d in range(1, chips)
+    ]
 
     for t in range(0, half, TILE):
         s = pl.ds(t, TILE)
         cbuf[:, s] = mm(pick, hi[:, s]) + mm(pick, lo[:, s])
     rs = [
         remote(
-            cbuf.at[rows_of((u + d) % n * n, n)], rbuf.at[d - 1],
-            rs_send.at[d - 1], rs_recv.at[d - 1], along_u(d),
-        )
-        for d in range(1, n)
+            cbuf.at[rows_of(other(d))], rbuf.at[d - 1],
+            rs_send.at[d - 1], rs_recv.at[d - 1], (other(d) * 2 + core, z),
+        )
+        for d in range(1, chips)
     ]
     for copy in rs:
         copy.start()
@@ -243,6 +205,24 @@
     def _():
         for copy in top_copies[EARLY:]:
             copy.start()
+
+    @pl.when(z != 0)
+    def _():
+        panel_z[0].wait_recv()
+
+    @pl.when(z == 0)
+    def _():
+        load_panel.wait()
+
+    @pl.when(core == 1)
+    def _():
+        to_zero.start()
+
+    @pl.when(me == 0)
+    def _():
+        for copy in l_copies:
+            copy.start()
+        l11[...] = pan[0]
 
     def forward(i):
         @pl.when((rank > 0) & (rank < chips - 1))
@@ -253,19 +233,6 @@
     proj[:, :] = fill
 
     forward(0)
-
-    @pl.when((core == 0) & (chip != 0))
-    def _():
-        l_first[0].wait_recv()
-
-    @pl.when((core == 0) & (chip != 0) & (y == 0))
-    def _():
-        for copy in l_then:
-            copy.start()
-
-    @pl.when(core == 0)
-    def _():
-        to_zero.wait_recv()
 
     levels = []
     size = 2
@@ -287,68 +254,38 @@
                 x = x - mm3(x, mm3(off_diagonal(size), x))
             kbuf[:B, :] = x
 
-    @pl.when(core == 0)
-    def _():
-        kbuf[:B, :] = jnp.where(eye, 1.0, 0.0) - off_diagonal(1)
-
-    cut = (len(levels) + 1) // 3
-    advance(levels[:cut])
+    forward(1)
     for copy in rs:
         copy.wait_recv()
-    total = cbuf[rows_of(u * n, n), :]
-    for d in range(1, n):
+    total = cbuf[rows_of(chip), :]
+    for d in range(1, chips):
         total = total + rbuf[d - 1]
-    hbuf[...] = total
-    hs = [
-        remote(
-            hbuf.at[rows_of((v + d) % n)], qbuf.at[d - 1],
-            hs_send.at[d - 1], hs_recv.at[d - 1], along_v(d),
-        )
-        for d in range(1, n)
-    ]
-    for copy in hs:
+    gbuf[rows_of(chip), :] = total
+    ag = [
+        remote(
+            gbuf.at[rows_of(chip)], gbuf.at[rows_of(chip)],
+            ag_send.at[d - 1], ag_recv.at[d - 1], (other(d) * 2 + core, z),
+        )
+        for d in range(1, chips)
+    ]
+    for copy in ag:
         copy.start()
-    forward(1)
-    advance(levels[cut : 2 * cut])
-    for copy in hs:
-        copy.wait_recv()
-    total = hbuf[rows_of(v), :]
-    for d in range(1, n):
-        total = total + qbuf[d - 1]
-    own_chunk = rows_of(u * n + v)
-    gbuf[own_chunk, :] = total
-
-    ag = [
-        remote(
-            gbuf.at[own_chunk], gbuf.at[own_chunk],
-            ag_send.at[d - 1], ag_recv.at[d - 1], along_v(d),
-        )
-        for d in range(1, n)
-    ]
-    fw = []
-    for e in range(n):
-        chunk = rows_of(u * n + (v - e + n) % n)
-        fw.append([
-            remote(
-                gbuf.at[chunk], gbuf.at[chunk],
-                fw_send.at[e * (n - 1) + d - 1], fw_recv.at[e * (n - 1) + d - 1],
-                along_u(d),
-            )
-            for d in range(1, n)
-        ])
-    for copy in ag + fw[0]:
-        copy.start()
-    for i in range(2, TOP_PIECES):
-        forward(i)
-    advance(levels[2 * cut :])
-    for e in range(1, n):
-        chunk = rows_of(u * n + (v - e + n) % n)
-        remote(
-            gbuf.at[chunk], gbuf.at[chunk],
-            ag_send.at[e - 1], ag_recv.at[e - 1], along_v(e),
-        ).wait_recv()
-        for copy in fw[e]:
-            copy.start()
+    forward(2)
+    forward(3)
+    @pl.when((core == 0) & (chip != 0))
+    def _():
+        l_copies[0].wait_recv()
+
+    @pl.when(core == 0)
+    def _():
+        to_zero.wait_recv()
+
+    @pl.when(core == 0)
+    def _():
+        kbuf[:B, :] = jnp.where(eye, 1.0, 0.0) - off_diagonal(1)
+
+    cut = 0
+    advance(levels[cut:])
 
     k_copy = remote(kbuf, kbuf, k_sem.at[0], k_sem.at[1], (peer, z))
 
@@ -379,14 +316,12 @@
 
     kh_peer, kl_peer = split(kbuf[peer_rows, :])
     kh_own, kl_own = split(kbuf[own_rows, :])
-    for e in range(n):
-        for d in range(1, n):
-            chunk = rows_of((u - d + n) % n * n + (v - e + n) % n)
-            remote(
-                gbuf.at[chunk], gbuf.at[chunk],
-                fw_send.at[e * (n - 1) + d - 1], fw_recv.at[e * (n - 1) + d - 1],
-                along_u(d),
-            ).wait_recv()
+    for d in range(1, chips):
+        came = rows_of((chip - d + chips) % chips)
+        remote(
+            gbuf.at[came], gbuf.at[came],
+            ag_send.at[d - 1], ag_recv.at[d - 1], (other(d) * 2 + core, z),
+        ).wait_recv()
 
     def tile_of(side, t):
         return pl.ds(pl.multiple_of(side * half + t, TILE), TILE)
@@ -400,12 +335,19 @@
         for t in tiles
     ]
     out_own = pltpu.make_async_copy(obuf.at[1], out_ref.at[:, mine], o_sem.at[0])
+    def keep_panel(slot, side, t):
+        if t == 0:
+            @pl.when((z == 0) & (core == 0))
+            def _():
+                obuf[slot, :, :B] = abuf[side, :, :B]
+
     for t in tiles:
         s = pl.ds(t, TILE)
         gh, gl = split(gbuf[:, s])
         obuf[0, :, s] = base[peer_rows, s] + (
             mm(kh_peer, gh) + (mm(kh_peer, gl) + mm(kl_peer, gh))
         )
+        keep_panel(0, 1 - core, t)
         out_peer[t // TILE].start()
     for t in tiles:
         s = pl.ds(t, TILE)
@@ -413,6 +355,7 @@
         obuf[1, :, s] = base[own_rows, s] + (
             mm(kh_own, gh) + (mm(kh_own, gl) + mm(kl_own, gh))
         )
+    keep_panel(1, core, 0)
     out_own.start()
 
     exchange.wait_send()
@@ -432,12 +375,7 @@
 
     @pl.when(me == 0)
     def _():
-        for copy in l_first:
-            copy.wait_send()
-
-    @pl.when((core == 0) & (y == 0))
-    def _():
-        for copy in l_then:
+        for copy in l_copies:
             copy.wait_send()
 
     @pl.when(rank < chips - 1)
@@ -445,7 +383,7 @@
         for copy in top_copies:
             copy.wait_send()
 
-    for copy in rs + hs + ag + [c for part in fw for c in part]:
+    for copy in rs + ag:
         copy.wait_send()
     out_own.wait()
     for t in tiles:
@@ -480,9 +418,7 @@
             pltpu.VMEM((2 * B, half), bf16),
             pltpu.VMEM((2 * B, half), bf16),
             pltpu.VMEM((B, half), f32),
-            pltpu.VMEM((n - 1, B // n, half), f32),
-            pltpu.VMEM((B // n, half), f32),
-            pltpu.VMEM((n - 1, B // chips, half), f32),
+            pltpu.VMEM((chips - 1, B // chips, half), f32),
             pltpu.VMEM((B, half), f32),
             pltpu.VMEM((2 * B, half), f32),
             pltpu.VMEM((2, B, half), f32),
@@ -495,17 +431,13 @@
             dma((cols_procs - 1,)),
             dma((1,)),
             dma((2,)),
-            dma((2 * (n - 1),)),
+            dma((chips - 1,)),
             dma((1,)),
             dma((2,)),
-            dma((n - 1,)),
-            dma((n - 1,)),
-            dma((n - 1,)),
-            dma((n - 1,)),
-            dma((n - 1,)),
-            dma((n - 1,)),
-            dma((n * (n - 1),)),
-            dma((n * (n - 1),)),
+            dma((chips - 1,)),
+            dma((chips - 1,)),
+            dma((chips - 1,)),
+            dma((chips - 1,)),
             dma((TOP_PIECES,)),
             dma((TOP_PIECES,)),
             dma((half // TILE,)),
@@ -513,12 +445,10 @@
             dma((1,)),
         ],
         compiler_params=pltpu.CompilerParams(
-            collective_id=0, has_side_effects=True, vmem_limit_bytes=60 * 1024 * 1024
+            collective_id=0, has_side_effects=True, vmem_limit_bytes=16 * 1024 * 1024
         ),
     )(matrix, pivots.reshape(1, -1))
-    col_ids = jnp.arange(cols, dtype=jnp.int32)
-    keep_panel = (lax.axis_index("pcol") == 0) & (col_ids < pivots.shape[0])
-    return jnp.where(keep_panel[None, :], matrix, stepped)
+    return stepped
 
 
 def solution(mesh):

time: 38.7 us -> 36.2 us (0.935)
  Pallas kernels: 36.2 us -> 33.2 us
  local copies, waits for them, and re-layouts: 0.01 us -> 2.85 us
  other arithmetic: 2.34 us -> 0 us
    pallas_call x1, Pallas kernels: 36.2 us -> 33.2 us  [local(): pl.pallas_call(functools.partial(kernel, procs, cols_procs, n), out_shape...]
    unnamed x2 -> x5, local copies, waits for them, and re-layouts: 0.01 us -> 2.85 us
    select_n x1 -> x0, other arithmetic: 2.33 us -> none  [local(): return jnp.where(keep_panel[None, :], matrix, stepped)]
where the time goes in v2:
time: 36.2 us; the launch traced here: 36.1 us
  Pallas kernels  33.2 us (92%)
  local copies, waits for them, and re-layouts  2.85 us (8%)
    pallas_call x1, Pallas kernels, local(): pl.pallas_call(functools.partial(kernel, procs, cols_procs, n), out_shape...  33.2 us
    unnamed x5, local copies, waits for them, and re-layouts  2.85 us

profile of v2, /device:TPU:29, one launch (start us, length us, event | category | flops | bytes accessed | tf_op | source)
XLA Modules:
  0.0 36.1 jit_solution(9725202806133597715)
XLA Ops:
  0.0 0.0 copy-start.1
  0.0 0.7 %copy-done.1 = s32[128]{0:T(128)S(1)} copy-done((s32[128]{0:T(128)S(1)}, s32[128]{0:T(128)}, u32[]{:S(2)}) %copy-start.1) | copy-done | bytes 536
  0.7 0.0 copy-start
  0.7 1.2 %copy-done = f32[128,2048]{1,0:T(8,128)S(1)} copy-done((f32[128,2048]{1,0:T(8,128)S(1)}, f32[128,2048]{1,0:T(8,128)}, u32[]{:S(2)}) %copy-start) | copy-done | bytes 1048600
  1.9 33.2 %shard_map.28 = f32[128,2048]{1,0:T(8,128)S(1)} custom-call(f32[128,2048]{1,0:T(8,128)S(1)} %copy-done, s32[1,128]{1,0:T(1,128)S(1)} %bitcast.1), custom_call_target="tpu_custom_call" | custom-call | tf_op jit(solution)/shard_map/pallas_call | solution.py:407
  35.1 1.0 %copy.4 = f32[128,2048]{1,0:T(8,128)} copy(f32[128,2048]{1,0:T(8,128)S(1)} %shard_map.28) | data formatting | bytes 2097152
Async XLA Ops:
  0.0 0.7 %copy-start.1 = (s32[128]{0:T(128)S(1)}, s32[128]{0:T(128)}, u32[]{:S(2)}) copy-start(s32[128]{0:T(128)} %param.3) | copy-start | bytes 1540
  0.7 1.2 %copy-start = (f32[128,2048]{1,0:T(8,128)S(1)}, f32[128,2048]{1,0:T(8,128)}, u32[]{:S(2)}) copy-start(f32[128,2048]{1,0:T(8,128)} %a_ref.1) | copy-start | bytes 3145732

commit v3 on v2

--- a/solution.py
+++ b/solution.py
@@ -9,7 +9,7 @@
 
 MESH = pl.DeviceIdType.MESH
 TOP_PIECES = 4
-EARLY = 2
+EARLY = 1
 TILE = 256
 
 

time: 36.2 us -> 37.3 us (1.030)
  the two profiles are of different devices: /device:TPU:29 before, /device:TPU:5 now
where the time goes in v3:
time: 37.3 us; the launch traced here: 37.1 us
  Pallas kernels  34.3 us (92%)
  local copies, waits for them, and re-layouts  2.85 us (8%)
    pallas_call x1, Pallas kernels, local(): pl.pallas_call(functools.partial(kernel, procs, cols_procs, n), out_shape...  34.3 us
    unnamed x5, local copies, waits for them, and re-layouts  2.85 us

profile of v3, /device:TPU:5, one launch (start us, length us, event | category | flops | bytes accessed | tf_op | source)
XLA Modules:
  0.0 37.1 jit_solution(497729908321166550)
XLA Ops:
  0.0 0.0 copy-start.1
  0.0 0.7 %copy-done.1 = s32[128]{0:T(128)S(1)} copy-done((s32[128]{0:T(128)S(1)}, s32[128]{0:T(128)}, u32[]{:S(2)}) %copy-start.1) | copy-done | bytes 536
  0.7 0.0 copy-start
  0.7 1.2 %copy-done = f32[128,2048]{1,0:T(8,128)S(1)} copy-done((f32[128,2048]{1,0:T(8,128)S(1)}, f32[128,2048]{1,0:T(8,128)}, u32[]{:S(2)}) %copy-start) | copy-done | bytes 1048600
  1.9 34.3 %shard_map.28 = f32[128,2048]{1,0:T(8,128)S(1)} custom-call(f32[128,2048]{1,0:T(8,128)S(1)} %copy-done, s32[1,128]{1,0:T(1,128)S(1)} %bitcast.1), custom_call_target="tpu_custom_call" | custom-call | tf_op jit(solution)/shard_map/pallas_call | solution.py:407
  36.2 1.0 %copy.4 = f32[128,2048]{1,0:T(8,128)} copy(f32[128,2048]{1,0:T(8,128)S(1)} %shard_map.28) | data formatting | bytes 2097152
Async XLA Ops:
  0.0 0.7 %copy-start.1 = (s32[128]{0:T(128)S(1)}, s32[128]{0:T(128)}, u32[]{:S(2)}) copy-start(s32[128]{0:T(128)} %param.3) | copy-start | bytes 1540
  0.7 1.2 %copy-start = (f32[128,2048]{1,0:T(8,128)S(1)}, f32[128,2048]{1,0:T(8,128)}, u32[]{:S(2)}) copy-start(f32[128,2048]{1,0:T(8,128)} %a_ref.1) | copy-start | bytes 3145732
